TPU v7x, 32 devices: a whole 2x2x4 slice. The times are simulated.
32 devices in a mesh: acq: 4 (over z), tile: 8 (over y, x, core).
Axes of the slice: x: 2, y: 2, z: 4, core: 2. Of those that a mesh axis runs over, the one named last changes fastest.
Arguments:
- slc_stack: bfloat16 [16, 2, 512, 1024], P('acq', None, 'tile'), may hold values from -6 to 6
- pair_list: int32 [48, 2], replicated, may hold values from 0 to 15, as said below
Outputs:
- filtered: float32 [48, 2, 128, 64], P('acq', None, 'tile')
Inputs may be any that keep to these rules, and one draw needn't show every extreme that they name: `pair_list`: the reference (first entry) of a pair owned by group g is one of group g's acquisitions, g * 4 to (g + 1) * 4 - 1; the secondary lies in another group. The pairs of one group use at most one secondary acquisition from each other group. No pair appears twice.
All inputs are finite; a program needn't handle non-finite values.
Results may differ from a plain program's by a relative error of at most 0.0003.
Values may be sent and summed in bfloat16 or wider, within the bound.
A program may use at most 128 MiB of HBM per device.

v0:
```python
import jax
import jax.numpy as jnp
from jax import lax
from jax.sharding import PartitionSpec as P

AZ_LOOKS = 4
RG_LOOKS = 16
PATCH = 32


def extended_2(block, sides, width):
    for axis, dim in sides:
        count = lax.axis_size(axis)
        forward = [(i, i + 1) for i in range(count - 1)]
        backward = [(target, source) for source, target in forward]
        low = lax.ppermute(
            lax.slice_in_dim(block, block.shape[dim] - width, None, axis=dim), axis, forward
        )
        high = lax.ppermute(lax.slice_in_dim(block, 0, width, axis=dim), axis, backward)
        block = jnp.concatenate([low, block, high], axis=dim)
    return block


def dft_tables(length):
    counter = jnp.arange(length, dtype=jnp.int32)
    product = counter[:, None] * counter[None, :] % length
    angles = product.astype(jnp.float32) * (2.0 * jnp.pi / length)
    return (jnp.cos(angles), jnp.sin(angles))


def taper_table(length):
    centre = (jnp.arange(length, dtype=jnp.float32) + 0.5) * (jnp.pi / length)
    profile = jnp.sin(centre) ** 2
    return profile[:, None] * profile[None, :]


def left_mult(matrix, blocks):
    return jnp.einsum("jk,...kl->...jl", matrix, blocks, precision=lax.Precision.HIGHEST)


def right_mult(blocks, matrix):
    return jnp.einsum("...jk,kl->...jl", blocks, matrix, precision=lax.Precision.HIGHEST)


def filter_patches(real_part, imag_part):
    length = real_part.shape[-1]
    cosine, sine_table = dft_tables(length)
    first_re = left_mult(cosine, real_part) + left_mult(sine_table, imag_part)
    first_im = left_mult(cosine, imag_part) - left_mult(sine_table, real_part)
    spec_re = right_mult(first_re, cosine) + right_mult(first_im, sine_table)
    spec_im = right_mult(first_im, cosine) - right_mult(first_re, sine_table)
    power_map = spec_re * spec_re + spec_im * spec_im
    smooth_rows = power_map + jnp.roll(power_map, 1, axis=-2) + jnp.roll(power_map, -1, axis=-2)
    smoothed = (
        smooth_rows + jnp.roll(smooth_rows, 1, axis=-1) + jnp.roll(smooth_rows, -1, axis=-1)
    ) / 9.0
    relative = smoothed / (jnp.mean(smoothed, axis=(-2, -1), keepdims=True) + 1e-06)
    weights = jnp.maximum(relative, 0.1) ** 0.25
    scaled_re = weights * spec_re
    scaled_im = weights * spec_im
    back_re = left_mult(cosine, scaled_re) - left_mult(sine_table, scaled_im)
    back_im = left_mult(cosine, scaled_im) + left_mult(sine_table, scaled_re)
    norm_factor = taper_table(length) / float(length * length)
    final_re = (right_mult(back_re, cosine) - right_mult(back_im, sine_table)) * norm_factor
    final_im = (right_mult(back_im, cosine) + right_mult(back_re, sine_table)) * norm_factor
    return (final_re, final_im)


def cut_patches(planes, half_patch):
    leading = planes.shape[:-2]
    row_count = planes.shape[-2] // half_patch - 1
    col_count = planes.shape[-1] // half_patch - 1
    blocks = planes.reshape(leading + (row_count + 1, half_patch, col_count + 1, half_patch))
    row_pairs = jnp.concatenate([blocks[..., :-1, :, :, :], blocks[..., 1:, :, :, :]], axis=-3)
    both_dims = jnp.concatenate([row_pairs[..., :-1, :], row_pairs[..., 1:, :]], axis=-1)
    return jnp.swapaxes(both_dims, -3, -2)


def join_columns(patches, half_patch):
    left_half = patches[..., :half_patch]
    right_half = patches[..., half_patch:]
    previous = jnp.concatenate(
        [jnp.zeros_like(right_half[..., :1, :, :]), right_half[..., :-1, :, :]], axis=-3
    )
    columns = jnp.swapaxes(left_half + previous, -3, -2)
    return columns.reshape(columns.shape[:-2] + (columns.shape[-2] * columns.shape[-1],))


def filter_grid(planes, half_patch):
    blocks = cut_patches(planes, half_patch)
    final_re, final_im = filter_patches(blocks[..., 0, :, :, :, :], blocks[..., 1, :, :, :, :])
    merged = jnp.stack([final_re, final_im], axis=-5)
    columns = join_columns(merged, half_patch)
    return (columns[..., :half_patch, :], columns[..., half_patch:, :])


def multilook(reference_slab, second_slab):
    ref_re = reference_slab[0].astype(jnp.float32)
    ref_im = reference_slab[1].astype(jnp.float32)
    sec_re = second_slab[0].astype(jnp.float32)
    sec_im = second_slab[1].astype(jnp.float32)
    stacked = jnp.stack([ref_re * sec_re + ref_im * sec_im, ref_im * sec_re - ref_re * sec_im])
    lines_in = stacked.shape[1]
    samples = stacked.shape[2]
    grouped = stacked.reshape(2, lines_in // AZ_LOOKS, AZ_LOOKS, samples // RG_LOOKS, RG_LOOKS)
    return jnp.mean(grouped, axis=(2, 4))


def per_device(slc_stack, pair_list):
    held_count = slc_stack.shape[0]
    groups = lax.axis_size("acq")
    member = lax.axis_index("acq")
    per_owner = pair_list.shape[0] // groups
    owners = jnp.arange(pair_list.shape[0], dtype=jnp.int32) // per_owner
    senders = pair_list[:, 1] // held_count
    group_ids = jnp.arange(groups, dtype=jnp.int32)
    matches = (owners[None, None, :] == group_ids[:, None, None]) & (
        senders[None, None, :] == group_ids[None, :, None]
    )
    wanted = jnp.max(jnp.where(matches, pair_list[None, None, :, 1], -1), axis=2)
    own_pairs = lax.dynamic_slice_in_dim(pair_list, member * per_owner, per_owner, 0)
    requests = lax.dynamic_index_in_dim(wanted, member, 0, keepdims=False)
    initial = jnp.zeros((groups,) + slc_stack.shape[1:], slc_stack.dtype)
    shard_rows = lax.all_gather(slc_stack, "acq", axis=0, tiled=True)
    inside = (requests >= 0) & (requests < shard_rows.shape[0])
    picked = jnp.take(shard_rows, jnp.clip(requests, 0, shard_rows.shape[0] - 1), axis=0)
    received = jnp.where(inside[:, None, None, None], picked, initial)
    local_refs = own_pairs[:, 0] - member * held_count
    remote_slots = own_pairs[:, 1] // held_count

    def look_pair(indices):
        reference_slab = lax.dynamic_index_in_dim(slc_stack, indices[0], 0, keepdims=False)
        second_slab = lax.dynamic_index_in_dim(received, indices[1], 0, keepdims=False)
        return multilook(reference_slab, second_slab)

    planes = lax.map(look_pair, jnp.stack([local_refs, remote_slots], axis=1))
    half_patch = PATCH // 2
    extended = extended_2(planes, (("tile", 2),), half_patch)
    padded = jnp.pad(extended, ((0, 0), (0, 0), (0, 0), (0, half_patch)))
    upper_half, lower_half = filter_grid(padded, half_patch)
    keep_first = (lax.axis_index("tile") > 0).astype(jnp.float32)
    lower_half = jnp.concatenate([lower_half[:, :, :1] * keep_first, lower_half[:, :, 1:]], axis=2)
    result = upper_half[:, :, 1:] + lower_half[:, :, :-1]
    return result.reshape(planes.shape)


def solution(mesh):
    return jax.shard_map(
        per_device,
        mesh=mesh,
        in_specs=(P("acq", None, "tile", None), P()),
        out_specs=P("acq", None, "tile", None),
        check_vma=False,
    )
```

profile of v0, /device:TPU:4, one launch (start us, length us, event | category | flops | bytes accessed | tf_op | source)
XLA Modules:
  0.0 279.1 jit_solution(8230051252422184918)
XLA Ops:
  9.7 81.2 %all-gather.2.cloned.1.call-done = bf16[16,2,64,1024]{3,2,1,0:T(8,128)(2,1)} async-done(((bf16[4,2,64,1024]{3,2,1,0:T(8,128)(2,1)}), bf16[16,2,64,1024]{3,2,1,0:T(8,128)(2,1)}) %all-gather.2.cloned.1.call-update) | async-done | bytes 4194320 | tf_op jit(solution)/shard_map/all_gather | solution.py:124
  91.0 2.8 %gather_fusion = bf16[4,2,64,1024]{3,2,1,0:T(8,128)(2,1)S(1)} fusion(bf16[16,2,64,1024]{3,2,1,0:T(8,128)(2,1)} %all-gather.2.cloned.1.call-done, s32[1024]{0:T(1024)S(1)} %pad_clamp_fusion), kind=kCustom, calls=%fused_computation | custom fusion | bytes 2097168 | tf_op jit(solution)/shard_map/jit(_take)/gather | solution.py:126
  94.9 105.7 %while.10 = (s32[]{:T(128)}, f32[12,2,16,64]{3,2,1,0:T(8,128)}, s32[12,2]{0,1:T(2,128)S(1)}, bf16[4,2,64,1024]{3,2,1,0:T(8,128)(2,1)}, bf16[4,2,64,1024]{3,2,1,0...) while((s32[]{:T(128)}, f32[12,2,16,64]{3,2,1,0:T(8,128)}, s32[12,2]{0,1:T(2,128)S(1)}, ...), condition=%wide.region_3.4_spmd, body=%wide.region_1.3_spmd.sunk | while | flops 917513 | bytes 3703017 | solution.py:136
  116.8 1.2 fusion.161
  125.6 1.2 fusion.161
  134.4 1.2 fusion.161
  200.6 2.8 collective-permute-start.1
  203.4 1.9 collective-permute-start
  205.4 1.6 collective-permute-done.1
  206.9 4.5 %collective-permute-done = f32[12,2,16,64]{3,2,1,0:T(8,128)S(1)} collective-permute-done((f32[12,2,16,64]{3,2,1,0:T(8,128)}, f32[12,2,16,64]{3,2,1,0:T(8,128)S(1)}, u32[]{:S(2)}, u32[]{:S(2)}) %collective-permute-start) | collective-permute-done | bytes 98336 | tf_op jit(solution)/shard_map/ppermute | solution.py:16
  212.5 2.6 reshape.332
  215.1 6.4 %fusion.152 = (f32[12,2,2,16,5,16]{5,4,3,2,1,0:T(8,128)}, f32[12,2,2,16,5,16]{5,4,3,2,1,0:T(8,128)}) fusion(f32[12,2,3,16,5,16]{5,4,3,2,1,0:T(8,128)} %reshape.332), kind=kLoop, calls=%fused_computation.190 | loop fusion | bytes 983040 | tf_op jit(solution)/shard_map/slice | solution.py:74
  221.4 2.2 copy.161
  223.7 3.4 %copy.160 = f32[12,2,2,16,5,16]{3,5,4,2,0,1:T(8,128)} copy(f32[12,2,2,16,5,16]{5,4,3,2,1,0:T(8,128)} %get-tuple-element.49) | data formatting | bytes 491520
  227.0 2.0 fusion.4
  229.8 1.4 fusion.37
  231.2 1.4 fusion.36
  232.7 1.4 convolution_subtract_fusion.1
  234.1 2.7 fusion.20
  236.8 2.7 fusion.18
  239.5 1.7 convolution_add_fusion.1
  241.2 2.6 fusion.26
  243.8 2.7 multiply_add_fusion
  249.0 1.2 fusion.149
  250.3 3.6 %fusion.42 = f32[12,2,4,32,32]{4,3,2,1,0:T(8,128)S(1)} fusion(f32[12,2,4,32,32]{4,3,2,1,0:T(8,128)S(1)} %fusion.26, f32[12,2,4,32,32]{4,3,2,1,0:T(8,128)S(1)} %get-tuple-element.44, f32[12,2,4]{2,1,0:T(2,128)S(1)} %multiply_add_fusion.1), kind=kOutput, calls=%fused_computation.62 | convolution fusion | flops 38057984 | bytes 1180032 | tf_op jit(solution)/shard_map/jk,...kl->...jl/dot_general | solution.py:38
  253.9 3.2 %fusion.38 = f32[12,2,4,32,32]{4,3,2,1,0:T(8,128)S(1)} fusion(f32[12,2,4,32,32]{4,3,2,1,0:T(8,128)S(1)} %get-tuple-element.64, f32[12,2,4,32,32]{4,3,2,1,0:T(8,128)S(1)} %get-tuple-element.44, f32[12,2,4]{2,1,0:T(2,128)S(1)} %multiply_add_fusion.1), kind=kOutput, calls=%fused_computation.58 | convolution fusion | flops 38057984 | bytes 1180032 | tf_op jit(solution)/shard_map/jk,...kl->...jl/dot_general | solution.py:38
  257.1 3.2 %convolution_add_fusion = f32[12,2,4,32,32]{4,3,2,1,0:T(8,128)S(1)} fusion(f32[12,2,4,32,32]{4,3,2,1,0:T(8,128)S(1)} %fusion.38, f32[12,2,4,32,32]{4,3,2,1,0:T(8,128)S(1)} %fusion.26, f32[12,2,4,32,32]{4,3,2,1,0:T(8,128)S(1)} %get-tuple-element.44, f32[12,2,4]{2,1,0:T(2,128)S(1)} %multiply_add_fusion.1), kind=kOutput, calls=%fused_computation.51 | convolution fusion | flops 38156288 | bytes 1573248 | tf_op jit(solution)/shard_map/jk,...kl->...jl/dot_general | solution.py:38
  260.4 1.5 fusion.12
  261.9 1.5 fusion.10
  263.5 3.4 %convolution_subtract_fusion = f32[12,2,4,32,32]{4,3,2,1,0:T(8,128)S(1)} fusion(f32[12,2,4,32,32]{4,3,2,1,0:T(8,128)S(1)} %fusion.42, f32[12,2,4,32,32]{4,3,2,1,0:T(8,128)S(1)} %get-tuple-element.64, f32[12,2,4,32,32]{4,3,2,1,0:T(8,128)S(1)} %get-tuple-element.44, f32[12,2,4]{2,1,0:T(2,128)S(1)} %multiply_add_fusion.1), kind=kOutput, calls=%fused_computation.52 | convolution fusion | flops 38156288 | bytes 1573248 | tf_op jit(solution)/shard_map/jk,...kl->...jl/dot_general | solution.py:38
  266.9 1.6 multiply_bitcast_fusion.1
  268.6 1.6 multiply_bitcast_fusion
  (138 shorter events, 68.8 us)
Async XLA Ops:
  6.5 84.4 %all-gather.2.cloned.1.call-start = ((), (), s32[]{:S(2)}) async-start(), calls=%async_computation | async-start | bytes 5242880 | tf_op jit(solution)/shard_map/all_gather | solution.py:124
  200.6 6.3 %collective-permute-start.1 = (f32[12,2,16,64]{3,2,1,0:T(8,128)}, f32[12,2,16,64]{3,2,1,0:T(8,128)S(1)}, u32[]{:S(2)}, u32[]{:S(2)}) collective-permute-start(f32[12,2,16,64]{3,2,1,0:T(8,128)} %get-tuple-element.32), channel_id=1, source_target_pairs={{1,0},{2,1},{3,2},{4,3},{5,4},{6,5},{7,6},{9,8},{10,9},{11,10},{12... | collective-permute-start | bytes 294920 | tf_op jit(solution)/shard_map/ppermute | solution.py:19
  203.4 8.1 %collective-permute-start = (f32[12,2,16,64]{3,2,1,0:T(8,128)}, f32[12,2,16,64]{3,2,1,0:T(8,128)S(1)}, u32[]{:S(2)}, u32[]{:S(2)}) collective-permute-start(f32[12,2,16,64]{3,2,1,0:T(8,128)} %get-tuple-element.32), channel_id=1, source_target_pairs={{0,1},{1,2},{2,3},{3,4},{4,5},{5,6},{6,7},{8,9},{9,10},{10,11},{11... | collective-permute-start | bytes 294920 | tf_op jit(solution)/shard_map/ppermute | solution.py:16
  227.0 2.0 copy-start
Sparse Core Ops, SparseCore 0:
  8.9 81.9 all-gather.1
where the time goes:
time: 284 us; the launch traced here: 279 us
  waiting for transfers between devices  88 us (31%)
  local copies, waits for them, and re-layouts  60 us (21%)
  loops' own time  43.6 us (15%)
  matrix products  36.6 us (13%)
  other arithmetic  32.2 us (11%)
  between operations  13.9 us (5%)
  starting transfers between devices  4.69 us (2%)
    all_gather x1, waiting for transfers between devices, per_device(): shard_rows = lax.all_gather(slc_stack, 'acq', axis=0, tiled=True)  81.2 us
    another operation x1, loops' own time, per_device(): planes = lax.map(look_pair, jnp.stack([local_refs, remote_slots], axis=1))  43.6 us
    dot_general x8, matrix products, left_mult(): jnp.einsum('jk,...kl->...jl', matrix, blocks, precision=lax.Precision.HIG...  19.6 us
    dot_general x8, matrix products, right_mult(): jnp.einsum('...jk,kl->...jl', blocks, matrix, precision=lax.Precision.HIG...  17 us
    add x24, local copies, waits for them, and re-layouts, multilook(): ref_re * sec_re + ref_im * sec_im  15.7 us
    sub x24, local copies, waits for them, and re-layouts, multilook(): ref_im * sec_re - ref_re * sec_im  15.6 us
    add x12, other arithmetic, multilook(): ref_re * sec_re + ref_im * sec_im  14.3 us
    dynamic_update_slice x12, other arithmetic, per_device(): planes = lax.map(look_pair, jnp.stack([local_refs, remote_slots], axis=1))  7.36 us
  transfers between devices with their start and end apart: 3, of which 3 were waited for; matrix products, arithmetic and copies ran while one was open for 1% of the time, Pallas kernels for 0%

commit v1 on v0

v1 whole, which is shorter than its diff:
```python
import functools

import jax
import jax.numpy as jnp
import ml_dtypes
import numpy as np
from jax import lax
from jax.experimental import pallas as pl
from jax.experimental.pallas import tpu as pltpu
from jax.sharding import PartitionSpec as P

AZ_LOOKS = 4
RG_LOOKS = 16
PATCH = 32
HALF = PATCH // 2
CHUNKS = 4
MESH = pl.DeviceIdType.MESH
BF16 = jnp.bfloat16
F32 = jnp.float32


def halves(matrix):
    high = matrix.astype(ml_dtypes.bfloat16)
    low = (matrix - high.astype(np.float64)).astype(ml_dtypes.bfloat16)
    return high, low


def tables(width):
    patches = width // HALF
    index = np.arange(PATCH)
    angle = 2.0 * np.pi * ((index[:, None] * index[None, :]) % PATCH) / PATCH
    cos, sin = np.cos(angle), np.sin(angle)
    taper = np.sin(np.pi * (index + 0.5) / PATCH) ** 2
    span = patches * PATCH
    forward = np.zeros((2 * width, 2 * span))
    backward = np.zeros((2 * span, 2 * width))
    for c in range(patches):
        for j in range(PATCH):
            n = c * HALF + j
            if n >= width:
                continue
            at = slice(c * PATCH, (c + 1) * PATCH)
            im = slice(span + c * PATCH, span + (c + 1) * PATCH)
            forward[n, at] = cos[j]
            forward[n, im] = -sin[j]
            forward[width + n, at] = sin[j]
            forward[width + n, im] = cos[j]
            backward[at, n] = cos[:, j] * taper[j]
            backward[im, n] = -sin[:, j] * taper[j]
            backward[at, width + n] = sin[:, j] * taper[j]
            backward[im, width + n] = cos[:, j] * taper[j]
    lines = np.block([[cos, sin], [-sin, cos]])
    scale = taper / float(PATCH * PATCH)
    inverse = np.block([[cos, -sin], [sin, cos]]) * np.concatenate([scale, scale])[:, None]
    upper = np.concatenate([inverse[:HALF], inverse[PATCH : PATCH + HALF]])
    lower = np.concatenate([inverse[HALF:PATCH], inverse[PATCH + HALF :]])
    inverse = np.concatenate([upper, lower], axis=1)
    ring = np.zeros((PATCH, PATCH))
    for k in range(PATCH):
        for step in (-1, 0, 1):
            ring[(k + step) % PATCH, k] = 1.0
    eye = np.eye(patches)
    smooth = np.concatenate([np.kron(eye, ring), np.kron(eye, np.ones((PATCH, PATCH)))], axis=1)

    fh, fl = halves(forward)
    lh, ll = halves(lines)
    ih, il = halves(inverse)
    bh, bl = halves(backward)
    sh = smooth.astype(ml_dtypes.bfloat16)
    return (
        np.concatenate([fh, fh, fl], axis=0),
        np.concatenate([lh, lh, ll], axis=1),
        np.concatenate([ih, ih, il], axis=1),
        np.concatenate([bh, bh, bl], axis=0),
        np.concatenate([sh, sh], axis=0),
    )


def line_order(lines):
    looks = lines // AZ_LOOKS
    order = np.zeros((lines, lines))
    for l in range(AZ_LOOKS):
        for look in range(looks):
            order[l * looks + look, look * AZ_LOOKS + l] = 1.0
    return order.astype(ml_dtypes.bfloat16)


def split(x):
    high = x.astype(BF16)
    return high, (x - high.astype(F32)).astype(BF16)


def mm(a, b):
    return jnp.dot(a, b, preferred_element_type=F32)


def kernel(
    groups, tiles, held, per_owner,
    pairs_ref, slc_ref, order_ref, fwd_ref, lines_ref, inv_ref, bwd_ref, smooth_ref,
    out_ref,
    own, stage, got, looks_w, planes, halo, result,
    send_sem, recv_sem, halo_send, halo_recv,
):
    me = lax.axis_index("acq")
    tile = lax.axis_index("tile")
    lines = slc_ref.shape[2]
    samples = slc_ref.shape[3]
    looks = lines // AZ_LOOKS
    width = samples // RG_LOOKS
    part = samples // CHUNKS
    span = (width // HALF) * PATCH
    left = lax.rem(tile + tiles - 1, tiles)
    right = lax.rem(tile + 1, tiles)

    barrier = pltpu.get_barrier_semaphore()
    for d in range(1, groups):
        pl.semaphore_signal(
            barrier, inc=1, device_id=(lax.rem(me + d, groups), tile), device_id_type=MESH
        )
    for other in (left, right):
        pl.semaphore_signal(barrier, inc=1, device_id=(me, other), device_id_type=MESH)

    for a in range(held):
        for plane in range(2):
            own[a, plane] = mm(order_ref[...], slc_ref[a, plane]).astype(BF16)

    distances = sorted(range(1, groups), key=lambda d: (abs(2 * d - groups), d))

    for d in distances:
        owner = lax.rem(me + d, groups)
        want = jnp.int32(0)
        for p in range(per_owner):
            second = pairs_ref[owner * per_owner + p, 1]
            inside = second - me * held
            want = jnp.where((inside >= 0) & (inside < held), inside, want)
        for q in range(CHUNKS):
            stage[d - 1, q] = own[want, :, :, q * part : (q + 1) * part]

    pl.semaphore_wait(barrier, groups + 1)

    def slab(d, q):
        return pltpu.make_async_remote_copy(
            src_ref=stage.at[d - 1, q],
            dst_ref=got.at[d - 1, q],
            send_sem=send_sem.at[d - 1, q],
            recv_sem=recv_sem.at[d - 1, q],
            device_id=(lax.rem(me + d, groups), tile),
            device_id_type=MESH,
        )

    for d in distances:
        for q in range(CHUNKS):
            slab(d, q).start()

    for q in range(CHUNKS):
        row = lax.broadcasted_iota(jnp.int32, (2 * part, 2 * width), 0)
        col = lax.broadcasted_iota(jnp.int32, (2 * part, 2 * width), 1)
        plane = jnp.where(row >= part, 1, 0)
        goal = plane * width + q * (part // RG_LOOKS) + (row - plane * part) // RG_LOOKS
        looks_w[q] = jnp.where(goal == col, 1.0 / (AZ_LOOKS * RG_LOOKS), 0.0).astype(BF16)

    def halo_copy(d, side):
        return pltpu.make_async_remote_copy(
            src_ref=planes.at[d - 1],
            dst_ref=halo.at[d - 1, side],
            send_sem=halo_send.at[d - 1, side],
            recv_sem=halo_recv.at[d - 1, side],
            device_id=(me, right if side == 0 else left),
            device_id_type=MESH,
        )

    def multilook(d):
        total = jnp.zeros((held * looks, 2 * width), F32)
        for q in range(CHUNKS):
            slab(d, q).wait_recv()
            at = slice(q * part, (q + 1) * part)
            re = [None] * held
            im = [None] * held
            for l in range(AZ_LOOKS):
                rows = slice(l * looks, (l + 1) * looks)
                br = got[d - 1, q, 0, rows, :].astype(F32)
                bi = got[d - 1, q, 1, rows, :].astype(F32)
                for a in range(held):
                    ar = own[a, 0, rows, at].astype(F32)
                    ai = own[a, 1, rows, at].astype(F32)
                    x = ar * br + ai * bi
                    y = ai * br - ar * bi
                    re[a] = x if l == 0 else re[a] + x
                    im[a] = y if l == 0 else im[a] + y
            both = jnp.concatenate(
                [jnp.concatenate(re, axis=0), jnp.concatenate(im, axis=0)], axis=1
            )
            high, low = split(both)
            total = total + mm(high, looks_w[q]) + mm(low, looks_w[q])
        planes[d - 1] = total

    def columns(x):
        high, low = split(x)
        return mm(jnp.concatenate([high, low, high], axis=1), fwd_ref[...])

    def filter_pairs(d):
        mid = columns(planes[d - 1])
        for side in range(2):
            halo_copy(d, side).wait_recv()
        low_part = columns(halo[d - 1, 0])
        later = jnp.where(tile == tiles - 1, 0.0, halo[d - 1, 1])
        high_part = columns(later)

        def patch(first, second, a):
            rows = slice(a * looks, (a + 1) * looks)
            return jnp.concatenate(
                [first[rows, :span], second[rows, :span], first[rows, span:], second[rows, span:]],
                axis=0,
            )

        blocks = [patch(mid, high_part, a) for a in range(held)]
        blocks += [patch(low_part, mid, a) for a in range(held)]
        high, low = split(jnp.concatenate(blocks, axis=1))
        spec = mm(lines_ref[...], jnp.concatenate([high, low, high], axis=0))
        spec_re, spec_im = spec[:PATCH], spec[PATCH:]
        power = spec_re * spec_re + spec_im * spec_im
        rows3 = power + pltpu.roll(power, 1, 0) + pltpu.roll(power, PATCH - 1, 0)
        stacked = jnp.concatenate(
            [rows3[:, i * span : (i + 1) * span] for i in range(2 * held)], axis=0
        )
        high, low = split(stacked)
        sums = mm(jnp.concatenate([high, low], axis=1), smooth_ref[...])
        weights = []
        for i in range(2 * held):
            block = sums[i * PATCH : (i + 1) * PATCH]
            smoothed = block[:, :span] * (1.0 / 9.0)
            mean = jnp.sum(block[:, span:], axis=0, keepdims=True) * (
                1.0 / (3.0 * PATCH * PATCH)
            )
            relative = smoothed / (mean + 1e-6)
            weight = jnp.sqrt(jnp.sqrt(jnp.maximum(relative, 0.1)))
            if i >= held:
                weight = jnp.where(tile == 0, 0.0, weight)
            weights.append(weight)
        weight = jnp.concatenate(weights, axis=1)
        scaled = jnp.concatenate([weight * spec_re, weight * spec_im], axis=0)
        scaled = jnp.concatenate([scaled[:, : held * span], scaled[:, held * span :]], axis=0)
        high, low = split(scaled)
        back = mm(inv_ref[...], jnp.concatenate([high, low, high], axis=0))
        back = jnp.concatenate(
            [
                jnp.concatenate(
                    [back[:HALF, a * span : (a + 1) * span], back[HALF:, a * span : (a + 1) * span]],
                    axis=1,
                )
                for a in range(held)
            ],
            axis=0,
        )
        high, low = split(back)
        final = mm(jnp.concatenate([high, low, high], axis=1), bwd_ref[...])
        for a in range(held):
            result[(d - 1) * held + a] = final[a * looks : (a + 1) * looks]

    before = None
    for d in distances:
        multilook(d)
        for side in range(2):
            halo_copy(d, side).start()
        if before is not None:
            filter_pairs(before)
        before = d
    filter_pairs(before)

    for p in range(per_owner):
        first = pairs_ref[me * per_owner + p, 0] - me * held
        source = pairs_ref[me * per_owner + p, 1] // held
        slot = lax.rem(me - source + groups, groups) - 1
        at = jnp.clip(slot * held + first, 0, (groups - 1) * held - 1)
        lines_out = result[at]
        out_ref[p, 0] = lines_out[:, :width]
        out_ref[p, 1] = lines_out[:, width:]

    for d in distances:
        for q in range(CHUNKS):
            slab(d, q).wait_send()
        for side in range(2):
            halo_copy(d, side).wait_send()


def per_device(groups, tiles, slc_stack, pair_list):
    held, _, lines, samples = slc_stack.shape
    per_owner = pair_list.shape[0] // groups
    looks, width = lines // AZ_LOOKS, samples // RG_LOOKS
    part = samples // CHUNKS
    others = groups - 1
    vmem = pl.BlockSpec(memory_space=pltpu.VMEM)
    smem = pl.BlockSpec(memory_space=pltpu.SMEM)
    constants = [jnp.asarray(t) for t in (line_order(lines),) + tables(width)]
    return pl.pallas_call(
        functools.partial(kernel, groups, tiles, held, per_owner),
        out_shape=jax.ShapeDtypeStruct((per_owner, 2, looks, width), F32),
        in_specs=[smem, vmem] + [vmem] * len(constants),
        out_specs=vmem,
        scratch_shapes=[
            pltpu.VMEM((held, 2, lines, samples), BF16),
            pltpu.VMEM((others, CHUNKS, 2, lines, part), BF16),
            pltpu.VMEM((others, CHUNKS, 2, lines, part), BF16),
            pltpu.VMEM((CHUNKS, 2 * part, 2 * width), BF16),
            pltpu.VMEM((others, held * looks, 2 * width), F32),
            pltpu.VMEM((others, 2, held * looks, 2 * width), F32),
            pltpu.VMEM((others * held, looks, 2 * width), F32),
            pltpu.SemaphoreType.DMA((others, CHUNKS)),
            pltpu.SemaphoreType.DMA((others, CHUNKS)),
            pltpu.SemaphoreType.DMA((others, 2)),
            pltpu.SemaphoreType.DMA((others, 2)),
        ],
        compiler_params=pltpu.CompilerParams(
            collective_id=0, has_side_effects=True, vmem_limit_bytes=48 * 2**20
        ),
    )(pair_list, slc_stack, *constants)


def solution(mesh):
    groups, tiles = mesh.shape["acq"], mesh.shape["tile"]
    return jax.shard_map(
        functools.partial(per_device, groups, tiles),
        mesh=mesh,
        in_specs=(P("acq", None, "tile", None), P()),
        out_specs=P("acq", None, "tile", None),
        check_vma=False,
    )
```

time: 284 us -> 42.1 us (0.15)
  the two profiles are of different devices: /device:TPU:4 before, /device:TPU:0 now
where the time goes in v1:
time: 42.1 us; the launch traced here: 41.7 us
  Pallas kernels  34.7 us (82%)
  local copies, waits for them, and re-layouts  6.91 us (16%)
    pallas_call x1, Pallas kernels, per_device(): pl.pallas_call(functools.partial(kernel, groups, tiles, held, per_owner),...  34.7 us
    unnamed x16, local copies, waits for them, and re-layouts  6.91 us

profile of v1, /device:TPU:0, one launch (start us, length us, event | category | flops | bytes accessed | tf_op | source)
XLA Modules:
  0.0 41.7 jit_solution(4322485174047686366)
XLA Ops:
  0.0 0.0 copy-start.5
  0.0 0.8 %copy.9.pairs_ref = s32[48,2]{1,0:T(8,128)S(1)} copy(s32[48,2]{0,1:T(2,128)} %param.9) | data formatting | bytes 768 | tf_op args[1]
  0.8 0.0 copy-done.5
  0.8 0.0 copy-start
  0.8 1.2 %copy-done = bf16[4,2,64,1024]{3,2,1,0:T(8,128)(2,1)S(1)} copy-done((bf16[4,2,64,1024]{3,2,1,0:T(8,128)(2,1)S(1)}, bf16[4,2,64,1024]{3,2,1,0:T(8,128)(2,1)}, u32[]{:S(2)}) %copy-start) | copy-done | bytes 1048600
  2.0 0.0 copy-start.1
  2.0 0.9 %copy-done.1 = bf16[768,128]{1,0:T(8,128)(2,1)S(1)} copy-done((bf16[768,128]{1,0:T(8,128)(2,1)S(1)}, bf16[768,128]{1,0:T(8,128)(2,1)}, u32[]{:S(2)}) %copy-start.1) | copy-done | bytes 196632
  2.9 0.0 copy-start.2
  2.9 0.9 %copy-done.2 = bf16[384,256]{1,0:T(8,128)(2,1)S(1)} copy-done((bf16[384,256]{1,0:T(8,128)(2,1)S(1)}, bf16[384,256]{1,0:T(8,128)(2,1)}, u32[]{:S(2)}) %copy-start.2) | copy-done | bytes 196632
  3.9 0.0 copy-start.3
  3.9 0.9 %copy-done.3 = bf16[256,256]{1,0:T(8,128)(2,1)S(1)} copy-done((bf16[256,256]{1,0:T(8,128)(2,1)S(1)}, bf16[256,256]{1,0:T(8,128)(2,1)}, u32[]{:S(2)}) %copy-start.3) | copy-done | bytes 131096
  4.8 0.0 copy-start.4
  4.8 0.8 %copy-done.4 = bf16[64,192]{1,0:T(8,128)(2,1)S(1)} copy-done((bf16[64,192]{1,0:T(8,128)(2,1)S(1)}, bf16[64,192]{1,0:T(8,128)(2,1)}, u32[]{:S(2)}) %copy-start.4) | copy-done | bytes 24600
  5.5 0.0 copy-start.6
  5.5 0.7 %copy-done.6 = bf16[64,64]{1,0:T(8,128)(2,1)S(1)} copy-done((bf16[64,64]{1,0:T(8,128)(2,1)S(1)}, bf16[64,64]{1,0:T(8,128)(2,1)}, u32[]{:S(2)}) %copy-start.6) | copy-done | bytes 8216
  6.2 34.7 %shard_map.82 = f32[12,2,16,64]{3,2,1,0:T(8,128)S(1)} custom-call(s32[48,2]{1,0:T(8,128)S(1)} %copy.9.pairs_ref, bf16[4,2,64,1024]{3,2,1,0:T(8,128)(2,1)S(1)} %copy-done, bf16[64,64]{1,0:T(8,128)(2,1)S(1)} %copy-done.6, bf16[384,256]{1,0:T(8,128)(2,1)S(1)} %copy-done.2, bf16[64,192]{1,0:T(8,128)(2,1)S(1)} %copy-done.4, bf16[32,384]{1,0:T(8,128)(2,1)S(1)} %copy-done.5, ...), custom_call_target="tpu_custom_call" | custom-call | tf_op jit(solution)/shard_map/pallas_call | solution.py:295
  41.0 0.7 %copy.11 = f32[12,2,16,64]{3,2,1,0:T(8,128)} copy(f32[12,2,16,64]{3,2,1,0:T(8,128)S(1)} %shard_map.82) | data formatting | bytes 196608
Async XLA Ops:
  0.0 0.8 %copy-start.5 = (bf16[32,384]{1,0:T(8,128)(2,1)S(1)}, bf16[32,384]{1,0:T(8,128)(2,1)}, u32[]{:S(2)}) copy-start(bf16[32,384]{1,0:T(8,128)(2,1)} %constant.15.clone.inv_ref) | copy-start | bytes 73732
  0.8 1.2 %copy-start = (bf16[4,2,64,1024]{3,2,1,0:T(8,128)(2,1)S(1)}, bf16[4,2,64,1024]{3,2,1,0:T(8,128)(2,1)}, u32[]{:S(2)}) copy-start(bf16[4,2,64,1024]{3,2,1,0:T(8,128)(2,1)} %slc_ref.1) | copy-start | bytes 3145732
  2.0 0.9 %copy-start.1 = (bf16[768,128]{1,0:T(8,128)(2,1)S(1)}, bf16[768,128]{1,0:T(8,128)(2,1)}, u32[]{:S(2)}) copy-start(bf16[768,128]{1,0:T(8,128)(2,1)} %constant.16.clone.bwd_ref) | copy-start | bytes 589828
  2.9 0.9 %copy-start.2 = (bf16[384,256]{1,0:T(8,128)(2,1)S(1)}, bf16[384,256]{1,0:T(8,128)(2,1)}, u32[]{:S(2)}) copy-start(bf16[384,256]{1,0:T(8,128)(2,1)} %constant.13.clone.fwd_ref) | copy-start | bytes 589828
  3.9 0.9 %copy-start.3 = (bf16[256,256]{1,0:T(8,128)(2,1)S(1)}, bf16[256,256]{1,0:T(8,128)(2,1)}, u32[]{:S(2)}) copy-start(bf16[256,256]{1,0:T(8,128)(2,1)} %constant.17.clone.smooth_ref) | copy-start | bytes 393220
  4.8 0.8 %copy-start.4 = (bf16[64,192]{1,0:T(8,128)(2,1)S(1)}, bf16[64,192]{1,0:T(8,128)(2,1)}, u32[]{:S(2)}) copy-start(bf16[64,192]{1,0:T(8,128)(2,1)} %constant.14.clone.lines_ref) | copy-start | bytes 73732
  5.5 0.7 %copy-start.6 = (bf16[64,64]{1,0:T(8,128)(2,1)S(1)}, bf16[64,64]{1,0:T(8,128)(2,1)}, u32[]{:S(2)}) copy-start(bf16[64,64]{1,0:T(8,128)(2,1)} %constant.12.clone.order_ref) | copy-start | bytes 24580

commit v2 on v1

--- a/solution.py
+++ b/solution.py
@@ -14,6 +14,7 @@
 PATCH = 32
 HALF = PATCH // 2
 CHUNKS = 4
+VMEM_LIMIT = 64 * 2**20 - 2**16
 MESH = pl.DeviceIdType.MESH
 BF16 = jnp.bfloat16
 F32 = jnp.float32
@@ -95,12 +96,14 @@
 
 
 def kernel(
-    groups, tiles, held, per_owner,
-    pairs_ref, slc_ref, order_ref, fwd_ref, lines_ref, inv_ref, bwd_ref, smooth_ref,
-    out_ref,
-    own, stage, got, looks_w, planes, halo, result,
-    send_sem, recv_sem, halo_send, halo_recv,
+    groups, tiles, held, per_owner, operands,
+    *refs,
 ):
+    inputs, (out_ref,), held_in = refs[:operands], refs[operands : operands + 1], refs[operands + 1 :]
+    copied, rest = held_in[:operands], held_in[operands:]
+    pairs_ref, slc_ref, order_ref, fwd_ref, lines_ref, inv_ref, bwd_ref, smooth_ref = copied
+    (own, stage, got, looks_w, planes, halo, result,
+     load_sem, send_sem, recv_sem, halo_send, halo_recv) = rest
     me = lax.axis_index("acq")
     tile = lax.axis_index("tile")
     lines = slc_ref.shape[2]
@@ -112,6 +115,13 @@
     left = lax.rem(tile + tiles - 1, tiles)
     right = lax.rem(tile + 1, tiles)
 
+    loads = [
+        pltpu.make_async_copy(source, target, load_sem.at[i])
+        for i, (source, target) in enumerate(zip(inputs, copied))
+    ]
+    for load in loads:
+        load.start()
+
     barrier = pltpu.get_barrier_semaphore()
     for d in range(1, groups):
         pl.semaphore_signal(
@@ -120,23 +130,21 @@
     for other in (left, right):
         pl.semaphore_signal(barrier, inc=1, device_id=(me, other), device_id_type=MESH)
 
-    for a in range(held):
-        for plane in range(2):
-            own[a, plane] = mm(order_ref[...], slc_ref[a, plane]).astype(BF16)
-
     distances = sorted(range(1, groups), key=lambda d: (abs(2 * d - groups), d))
 
+    def permuted(x):
+        return mm(order_ref[...], x).astype(BF16)
+
+    loads[0].wait()
+    wants = {}
     for d in distances:
         owner = lax.rem(me + d, groups)
         want = jnp.int32(0)
         for p in range(per_owner):
-            second = pairs_ref[owner * per_owner + p, 1]
+            second = pairs_ref[1, owner * per_owner + p]
             inside = second - me * held
             want = jnp.where((inside >= 0) & (inside < held), inside, want)
-        for q in range(CHUNKS):
-            stage[d - 1, q] = own[want, :, :, q * part : (q + 1) * part]
-
-    pl.semaphore_wait(barrier, groups + 1)
+        wants[d] = want
 
     def slab(d, q):
         return pltpu.make_async_remote_copy(
@@ -148,9 +156,27 @@
             device_id_type=MESH,
         )
 
-    for d in distances:
+    def fill(d, q):
+        for plane in range(2):
+            stage[d - 1, q, plane] = permuted(
+                slc_ref[wants[d], plane, :, q * part : (q + 1) * part]
+            )
+
+    loads[1].wait()
+    loads[2].wait()
+    for q in range(CHUNKS):
+        fill(distances[0], q)
+    pl.semaphore_wait(barrier, groups + 1)
+    for q in range(CHUNKS):
+        slab(distances[0], q).start()
+    for d in distances[1:]:
         for q in range(CHUNKS):
+            fill(d, q)
             slab(d, q).start()
+
+    for a in range(held):
+        for plane in range(2):
+            own[a, plane] = permuted(slc_ref[a, plane])
 
     for q in range(CHUNKS):
         row = lax.broadcasted_iota(jnp.int32, (2 * part, 2 * width), 0)
@@ -257,6 +283,9 @@
         for a in range(held):
             result[(d - 1) * held + a] = final[a * looks : (a + 1) * looks]
 
+    for load in loads[3:]:
+        load.wait()
+
     before = None
     for d in distances:
         multilook(d)
@@ -268,8 +297,8 @@
     filter_pairs(before)
 
     for p in range(per_owner):
-        first = pairs_ref[me * per_owner + p, 0] - me * held
-        source = pairs_ref[me * per_owner + p, 1] // held
+        first = pairs_ref[0, me * per_owner + p] - me * held
+        source = pairs_ref[1, me * per_owner + p] // held
         slot = lax.rem(me - source + groups, groups) - 1
         at = jnp.clip(slot * held + first, 0, (groups - 1) * held - 1)
         lines_out = result[at]
@@ -289,15 +318,16 @@
     looks, width = lines // AZ_LOOKS, samples // RG_LOOKS
     part = samples // CHUNKS
     others = groups - 1
-    vmem = pl.BlockSpec(memory_space=pltpu.VMEM)
-    smem = pl.BlockSpec(memory_space=pltpu.SMEM)
     constants = [jnp.asarray(t) for t in (line_order(lines),) + tables(width)]
+    operands = [pair_list.T, slc_stack] + constants
     return pl.pallas_call(
-        functools.partial(kernel, groups, tiles, held, per_owner),
+        functools.partial(kernel, groups, tiles, held, per_owner, len(operands)),
         out_shape=jax.ShapeDtypeStruct((per_owner, 2, looks, width), F32),
-        in_specs=[smem, vmem] + [vmem] * len(constants),
-        out_specs=vmem,
+        in_specs=[pl.BlockSpec(memory_space=pltpu.HBM)] * len(operands),
+        out_specs=pl.BlockSpec(memory_space=pltpu.VMEM),
         scratch_shapes=[
+            pltpu.SMEM(pair_list.shape[::-1], pair_list.dtype),
+            *[pltpu.VMEM(x.shape, x.dtype) for x in operands[1:]],
             pltpu.VMEM((held, 2, lines, samples), BF16),
             pltpu.VMEM((others, CHUNKS, 2, lines, part), BF16),
             pltpu.VMEM((others, CHUNKS, 2, lines, part), BF16),
@@ -305,15 +335,16 @@
             pltpu.VMEM((others, held * looks, 2 * width), F32),
             pltpu.VMEM((others, 2, held * looks, 2 * width), F32),
             pltpu.VMEM((others * held, looks, 2 * width), F32),
+            pltpu.SemaphoreType.DMA((len(operands),)),
             pltpu.SemaphoreType.DMA((others, CHUNKS)),
             pltpu.SemaphoreType.DMA((others, CHUNKS)),
             pltpu.SemaphoreType.DMA((others, 2)),
             pltpu.SemaphoreType.DMA((others, 2)),
         ],
         compiler_params=pltpu.CompilerParams(
-            collective_id=0, has_side_effects=True, vmem_limit_bytes=48 * 2**20
+            collective_id=0, has_side_effects=True, vmem_limit_bytes=VMEM_LIMIT
         ),
-    )(pair_list, slc_stack, *constants)
+    )(*operands)
 
 
 def solution(mesh):

time: 42.1 us -> 36.2 us (0.86)
  local copies, waits for them, and re-layouts: 6.91 us -> 1.62 us
    unnamed x16 -> x1, local copies, waits for them, and re-layouts: 6.91 us -> 1.62 us
where the time goes in v2:
time: 36.2 us; the launch traced here: 36 us
  Pallas kernels  34.4 us (95%)
  local copies, waits for them, and re-layouts  1.62 us (4%)
    pallas_call x1, Pallas kernels, per_device(): pl.pallas_call(functools.partial(kernel, groups, tiles, held, per_owner,...  34.4 us
    unnamed x1, local copies, waits for them, and re-layouts  1.62 us

profile of v2, /device:TPU:0, one launch (start us, length us, event | category | flops | bytes accessed | tf_op | source)
XLA Modules:
  0.0 36.0 jit_solution(3453581162891127014)
XLA Ops:
  0.0 34.4 %shard_map.82 = f32[12,2,16,64]{3,2,1,0:T(8,128)} custom-call(s32[2,48]{1,0:T(2,128)} %bitcast.1, bf16[4,2,64,1024]{3,2,1,0:T(8,128)(2,1)} %refs_1_.1, bf16[64,64]{1,0:T(8,128)(2,1)} %constant.12.clone.refs_2_, bf16[384,256]{1,0:T(8,128)(2,1)} %constant.13.clone.refs_3_, bf16[64,192]{1,0:T(8,128)(2,1)} %constant.14.clone.refs_4_, ...), custom_call_target="tpu_custom_call" | custom-call | tf_op jit(solution)/shard_map/pallas_call | solution.py:323
  34.4 1.6 %copy.10 = f32[12,2,16,64]{3,2,1,0:T(8,128)} copy(f32[12,2,16,64]{3,2,1,0:T(8,128)} %shard_map.82) | data formatting | bytes 196608

commit v3 on v2

--- a/solution.py
+++ b/solution.py
@@ -13,7 +13,7 @@
 RG_LOOKS = 16
 PATCH = 32
 HALF = PATCH // 2
-CHUNKS = 4
+CHUNKS = 2
 VMEM_LIMIT = 64 * 2**20 - 2**16
 MESH = pl.DeviceIdType.MESH
 BF16 = jnp.bfloat16
@@ -77,13 +77,13 @@
     )
 
 
-def line_order(lines):
-    looks = lines // AZ_LOOKS
-    order = np.zeros((lines, lines))
-    for l in range(AZ_LOOKS):
-        for look in range(looks):
-            order[l * looks + look, look * AZ_LOOKS + l] = 1.0
-    return order.astype(ml_dtypes.bfloat16)
+def packed(parts):
+    wide = max(x.shape[1] for x in parts)
+    starts = np.cumsum([0] + [x.shape[0] for x in parts])
+    whole = np.zeros((starts[-1], wide), ml_dtypes.bfloat16)
+    for start, x in zip(starts, parts):
+        whole[start : start + x.shape[0], : x.shape[1]] = x
+    return whole, [(int(start), *x.shape) for start, x in zip(starts, parts)]
 
 
 def split(x):
@@ -96,12 +96,15 @@
 
 
 def kernel(
-    groups, tiles, held, per_owner, operands,
+    groups, tiles, held, per_owner, places, operands,
     *refs,
 ):
     inputs, (out_ref,), held_in = refs[:operands], refs[operands : operands + 1], refs[operands + 1 :]
     copied, rest = held_in[:operands], held_in[operands:]
-    pairs_ref, slc_ref, order_ref, fwd_ref, lines_ref, inv_ref, bwd_ref, smooth_ref = copied
+    pairs_ref, slc_ref, tables_ref = copied
+    fwd_ref, lines_ref, inv_ref, bwd_ref, smooth_ref = [
+        tables_ref.at[start : start + rows, :columns] for start, rows, columns in places
+    ]
     (own, stage, got, looks_w, planes, halo, result,
      load_sem, send_sem, recv_sem, halo_send, halo_recv) = rest
     me = lax.axis_index("acq")
@@ -132,8 +135,13 @@
 
     distances = sorted(range(1, groups), key=lambda d: (abs(2 * d - groups), d))
 
+    row = lax.broadcasted_iota(jnp.int32, (lines, lines), 0)
+    col = lax.broadcasted_iota(jnp.int32, (lines, lines), 1)
+    origin = (row % looks) * AZ_LOOKS + row // looks
+    order = jnp.where(origin == col, 1.0, 0.0).astype(BF16)
+
     def permuted(x):
-        return mm(order_ref[...], x).astype(BF16)
+        return mm(order, x).astype(BF16)
 
     loads[0].wait()
     wants = {}
@@ -163,7 +171,6 @@
             )
 
     loads[1].wait()
-    loads[2].wait()
     for q in range(CHUNKS):
         fill(distances[0], q)
     pl.semaphore_wait(barrier, groups + 1)
@@ -283,18 +290,15 @@
         for a in range(held):
             result[(d - 1) * held + a] = final[a * looks : (a + 1) * looks]
 
-    for load in loads[3:]:
+    for load in loads[2:]:
         load.wait()
 
-    before = None
     for d in distances:
         multilook(d)
         for side in range(2):
             halo_copy(d, side).start()
-        if before is not None:
-            filter_pairs(before)
-        before = d
-    filter_pairs(before)
+    for d in distances:
+        filter_pairs(d)
 
     for p in range(per_owner):
         first = pairs_ref[0, me * per_owner + p] - me * held
@@ -318,10 +322,10 @@
     looks, width = lines // AZ_LOOKS, samples // RG_LOOKS
     part = samples // CHUNKS
     others = groups - 1
-    constants = [jnp.asarray(t) for t in (line_order(lines),) + tables(width)]
-    operands = [pair_list.T, slc_stack] + constants
+    constants, places = packed(tables(width))
+    operands = [pair_list.T, slc_stack, jnp.asarray(constants)]
     return pl.pallas_call(
-        functools.partial(kernel, groups, tiles, held, per_owner, len(operands)),
+        functools.partial(kernel, groups, tiles, held, per_owner, places, len(operands)),
         out_shape=jax.ShapeDtypeStruct((per_owner, 2, looks, width), F32),
         in_specs=[pl.BlockSpec(memory_space=pltpu.HBM)] * len(operands),
         out_specs=pl.BlockSpec(memory_space=pltpu.VMEM),

time: 36.2 us -> 34.7 us (0.959)
  the two profiles are of different devices: /device:TPU:0 before, /device:TPU:17 now
where the time goes in v3:
time: 34.7 us; the launch traced here: 34.5 us
  Pallas kernels  32.9 us (95%)
  local copies, waits for them, and re-layouts  1.62 us (5%)
    pallas_call x1, Pallas kernels, per_device(): pl.pallas_call(functools.partial(kernel, groups, tiles, held, per_owner,...  32.9 us
    unnamed x1, local copies, waits for them, and re-layouts  1.62 us

profile of v3, /device:TPU:17, one launch (start us, length us, event | category | flops | bytes accessed | tf_op | source)
XLA Modules:
  0.0 34.5 jit_solution(9212542558173891379)
XLA Ops:
  0.0 32.9 %shard_map.37 = f32[12,2,16,64]{3,2,1,0:T(8,128)} custom-call(s32[2,48]{1,0:T(2,128)} %bitcast.1, bf16[4,2,64,1024]{3,2,1,0:T(8,128)(2,1)} %refs_1_.1, bf16[1504,384]{1,0:T(8,128)(2,1)} %constant.2.clone.refs_2_), custom_call_target="tpu_custom_call" | custom-call | tf_op jit(solution)/shard_map/pallas_call | solution.py:327
  32.9 1.6 %copy.5 = f32[12,2,16,64]{3,2,1,0:T(8,128)} copy(f32[12,2,16,64]{3,2,1,0:T(8,128)} %shard_map.37) | data formatting | bytes 196608
